TPU v7x, 256 devices: a whole 4x4x8 slice. The times are simulated.
256 devices in a mesh: seq: 32 (over z, y), fsdp: 8 (over x, core).
Axes of the slice: x: 4, y: 4, z: 8, core: 2. Of those that a mesh axis runs over, the one named last changes fastest.
Arguments:
- queries: bfloat16 [32, 8, 256, 2560], P('seq', 'fsdp'), may hold values from -6 to 6
- key_rows: bfloat16 [32, 8, 256, 2560], P('seq', 'fsdp'), may hold values from -6 to 6
- value_rows: bfloat16 [32, 8, 256, 2560], P('seq', 'fsdp'), may hold values from -6 to 6
- cache_keys: bfloat16 [32, 4, 8, 64, 2560], P('seq', None, 'fsdp'), may hold values from -6 to 6
- cache_values: bfloat16 [32, 4, 8, 64, 2560], P('seq', None, 'fsdp'), may hold values from -6 to 6
- cache_frames: int32 [4, 8], P(None, 'fsdp'), may hold values from 1 to 8, as said below
- neighbors: int32 [32, 9], replicated, may hold values from 0 to 31, as said below
- tile_order: int32 [32], replicated, may hold values from 0 to 31, each once
- out_weight: bfloat16 [2560, 5120], P('fsdp', 'seq'), may hold values from -0.125 to 0.125
Outputs:
- block_output: bfloat16 [32, 8, 256, 5120], P('seq', 'fsdp')
Inputs may be any that keep to these rules, and one draw needn't show every extreme that they name: The last cache_frames[b, g] of the 8 cache frames are live for trajectory (b, g); some trajectory has all 8, and the counts are not all equal. `neighbors`: row t names 9 different tiles of the frame, t itself first; tiles lie on a grid in rows of 8. `tile_order`: each tile stands in exactly one slot.
All inputs are finite; a program needn't handle non-finite values.
Results may differ from a plain program's by a relative error of at most 0.017.
Values may be sent and summed in bfloat16 or wider, within the bound.
A program may use at most 128 MiB of HBM per device.

v0:
```python
import jax
import jax.numpy as jnp
from jax import lax
from jax.sharding import PartitionSpec as P

HEADS = 20
HD = 128
TILE = 8
SPAN = 8
CACHE = 8


def normalized(scores):
    top = jnp.max(scores, axis=-1, keepdims=True)
    weights = jnp.exp(scores - top)
    return (weights / jnp.sum(weights, axis=-1, keepdims=True)).astype(jnp.bfloat16)


def shards(
    queries,
    key_rows,
    value_rows,
    cache_keys,
    cache_values,
    cache_frames,
    neighbors,
    tile_order,
    out_weight,
):
    tile_count = neighbors.shape[0]
    token_count = tile_count * TILE
    feature_count = HEADS * HD
    frame_q = queries.reshape(token_count, HEADS, HD)
    frame_k = key_rows.reshape(token_count, HEADS, HD)
    frame_v = value_rows.reshape(token_count, HEADS, HD)
    tile_ids = jnp.arange(tile_count, dtype=jnp.int32)
    near_tiles = jnp.any(neighbors[:, :, None] == tile_ids[None, None, :], axis=1)
    token_tile = jnp.arange(token_count, dtype=jnp.int32) // TILE
    near_tokens = jnp.take(jnp.take(near_tiles, token_tile, axis=0), token_tile, axis=1)
    spatial_scores = jnp.einsum(
        "qhd,khd->hqk", frame_q, frame_k, preferred_element_type=jnp.float32
    ) * HD ** (-0.5)
    spatial_scores = jnp.where(near_tokens[None], spatial_scores, -jnp.inf)
    spatial_probs = normalized(spatial_scores)
    spatial_out = jnp.einsum(
        "hqk,khd->qhd", spatial_probs, frame_v, preferred_element_type=jnp.float32
    ).astype(jnp.bfloat16)
    ordered_q = jnp.take(queries.reshape(tile_count, TILE, feature_count), tile_order, axis=0)[None]
    ordered_k = jnp.take(key_rows.reshape(tile_count, TILE, feature_count), tile_order, axis=0)[
        None
    ]
    ordered_v = jnp.take(value_rows.reshape(tile_count, TILE, feature_count), tile_order, axis=0)[
        None
    ]
    moved_q, moved_k, moved_v = (
        lax.all_to_all(ordered_q, "seq", split_axis=1, concat_axis=0, tiled=True),
        lax.all_to_all(ordered_k, "seq", split_axis=1, concat_axis=0, tiled=True),
        lax.all_to_all(ordered_v, "seq", split_axis=1, concat_axis=0, tiled=True),
    )
    source_count = moved_q.shape[0]
    slot_count = moved_q.shape[1]
    groups = cache_frames.shape[0]
    span_rows = SPAN * TILE
    cache_rows = CACHE * TILE

    def slot_major(moved):
        return (
            moved.reshape(groups, SPAN, slot_count, TILE, HEADS, HD)
            .transpose(0, 2, 1, 3, 4, 5)
            .reshape(groups, slot_count, span_rows, HEADS, HD)
        )

    slot_q = slot_major(moved_q)
    slot_k = slot_major(moved_k)
    slot_v = slot_major(moved_v)
    stored_keys = cache_keys.reshape(slot_count, groups, cache_rows, HEADS, HD).transpose(
        1, 0, 2, 3, 4
    )
    stored_values = cache_values.reshape(slot_count, groups, cache_rows, HEADS, HD).transpose(
        1, 0, 2, 3, 4
    )
    joined_keys = jnp.concatenate([stored_keys, slot_k], axis=2)
    joined_values = jnp.concatenate([stored_values, slot_v], axis=2)
    temporal_scores = jnp.einsum(
        "buqhd,bukhd->buhqk", slot_q, joined_keys, preferred_element_type=jnp.float32
    ) * HD ** (-0.5)
    key_index = jnp.arange(cache_rows + span_rows, dtype=jnp.int32)
    query_frame = jnp.arange(span_rows, dtype=jnp.int32) // TILE
    cache_live = (key_index[None, :] < cache_rows) & (
        key_index[None, :] // TILE >= (CACHE - cache_frames[:, 0])[:, None]
    )
    span_live = (key_index[None, :] >= cache_rows) & (
        (key_index[None, :] - cache_rows) // TILE <= query_frame[:, None]
    )
    live = cache_live[:, None, :] | span_live[None, :, :]
    temporal_scores = jnp.where(live[:, None, None], temporal_scores, -jnp.inf)
    temporal_probs = normalized(temporal_scores)
    temporal = jnp.einsum(
        "buhqk,bukhd->buqhd", temporal_probs, joined_values, preferred_element_type=jnp.float32
    )
    temporal = temporal.astype(jnp.bfloat16).reshape(groups, slot_count, SPAN, TILE, HEADS, HD)
    temporal_out = temporal.transpose(0, 2, 1, 3, 4, 5).reshape(
        source_count, slot_count, TILE, feature_count
    )
    returned = lax.all_to_all(temporal_out, "seq", split_axis=0, concat_axis=1, tiled=True)
    inverse = jnp.sum(
        jnp.where(tile_order[None, :] == tile_ids[:, None], tile_ids[None, :], 0), axis=1
    )
    temporal_frame = jnp.take(returned[0], inverse, axis=0)
    combined = (
        spatial_out.reshape(token_count, feature_count).astype(jnp.float32)
        + temporal_frame.reshape(token_count, feature_count).astype(jnp.float32)
    ).astype(jnp.bfloat16)
    weight_block = lax.all_gather(out_weight, "fsdp", axis=0, tiled=True)
    projected = jnp.dot(
        combined,
        lax.all_gather(weight_block, "seq", axis=1, tiled=True),
        preferred_element_type=jnp.float32,
    )
    return projected.astype(jnp.bfloat16).reshape(1, 1, token_count, projected.shape[1])


def solution(mesh):
    placed = (
        P("seq", "fsdp", None, None),
        P("seq", "fsdp", None, None),
        P("seq", "fsdp", None, None),
        P("seq", None, "fsdp", None, None),
        P("seq", None, "fsdp", None, None),
        P(None, "fsdp"),
        P(),
        P(),
        P("fsdp", "seq"),
    )
    return jax.shard_map(
        shards, mesh=mesh, in_specs=placed, out_specs=P("seq", "fsdp", None, None), check_vma=False
    )
```

profile of v0, /device:TPU:1, one launch (start us, length us, event | category | flops | bytes accessed | tf_op | source)
XLA Modules:
  0.0 331.8 jit_solution(5121339735521082161)
XLA Ops:
  6.5 17.0 %all-gather = bf16[8,320,160]{1,2,0:T(8,128)(2,1)S(1)} all-gather(bf16[1,320,160]{1,2,0:T(8,128)(2,1)} %bitcast.79), channel_id=1, replica_groups=mesh['seq'=32,'fsdp'=8] {'fsdp'}, dimensions={0}, use_global_device_ids=true | all-gather | bytes 921600 | tf_op jit(solution)/shard_map/all_gather | solution.py:114
  23.9 1.6 reshape.391
  25.6 1.7 gather_fusion.2
  27.2 1.7 gather_fusion.3
  28.9 1.7 gather_fusion.4
  30.6 3.6 %select_bitcast_fusion.1 = (bf16[1,32,8,2560]{3,2,0,1:T(8,128)(2,1)}, bf16[1,32,8,2560]{3,2,0,1:T(8,128)(2,1)S(1)}, bf16[1,32,8,2560]{3,2,0,1:T(8,128)(2,1)S(1)}) fusion(bf16[32,8,2560]{2,1,0:T(8,128)(2,1)} %gather_fusion.3, pred[32]{0:T(512)(128)(4,1)S(1)} %compare_and_fusion.2, bf16[32,8,2560]{2,1,0:T(8,128)(2,1)} %gather_fusion.4, ...), kind=kLoop, calls=%fused_computation.40 | loop fusion | flops 1966080 | bytes 7864352 | tf_op jit(solution)/shard_map/broadcast_in_dim | solution.py:48
  34.2 58.4 %all_to_all.16 = bf16[1,32,8,2560]{3,2,0,1:T(8,128)(2,1)} all-to-all(bf16[1,32,8,2560]{3,2,0,1:T(8,128)(2,1)S(1)} %get-tuple-element.7), channel_id=1, replica_groups=mesh['seq'=32,'fsdp'=8] {'seq'}, dimensions={1} | all-to-all | bytes 2621440 | tf_op jit(solution)/shard_map/all_to_all | solution.py:57
  92.6 40.9 %all_to_all.17 = bf16[1,32,8,2560]{3,2,0,1:T(8,128)(2,1)} all-to-all(bf16[1,32,8,2560]{3,2,0,1:T(8,128)(2,1)S(1)} %get-tuple-element.8), channel_id=1, replica_groups=mesh['seq'=32,'fsdp'=8] {'seq'}, dimensions={1} | all-to-all | bytes 2621440 | tf_op jit(solution)/shard_map/all_to_all | solution.py:58
  133.5 4.9 %all-to-all-start.1 = ((bf16[1,32,8,2560]{3,2,0,1:T(8,128)(2,1)}), bf16[1,32,8,2560]{3,2,0,1:T(8,128)(2,1)}, u32[]{:S(2)}, u32[]{:S(2)}) async-start(bf16[1,32,8,2560]{3,2,0,1:T(8,128)(2,1)} %get-tuple-element.6), calls=%async_computation.1 | async-start | bytes 2621440 | tf_op jit(solution)/shard_map/all_to_all | solution.py:56
  145.0 2.5 transpose_reshape.6
  154.0 31.1 %all-to-all-done.1 = bf16[1,32,8,2560]{3,2,0,1:T(8,128)(2,1)} async-done(((bf16[1,32,8,2560]{3,2,0,1:T(8,128)(2,1)}), bf16[1,32,8,2560]{3,2,0,1:T(8,128)(2,1)}, u32[]{:S(2)}, u32[]{:S(2)}) %all-to-all-start.1) | async-done | bytes 1310752 | tf_op jit(solution)/shard_map/all_to_all | solution.py:56
  185.1 2.6 reshape.332
  187.6 3.2 fusion.4
  190.8 1.5 copy-done.7
  194.1 11.2 %fusion.19 = bf16[4,1,64,20,128]{4,2,3,0,1:T(8,128)(2,1)} fusion(bf16[4,1,64,20,128]{4,2,3,0,1:T(8,128)(2,1)S(1)} %copy-done.11, bf16[4,1,64,20,128]{4,2,3,0,1:T(8,128)(2,1)S(1)} %copy-done.10, f32[4,20,64]{2,1,0:T(8,128)S(1)} %fusion.45, f32[4,20,64,128]{3,2,1,0:T(8,128)} %copy-done.7, pred[4,64,128]{2,1,0:T(8,128)(4,1)S(1)} %broadcast_or_fusion), kind=kOutput, calls=%fused_computation.35 | convolution fusion | flops 176952448 | bytes 6606848 | tf_op jit(solution)/shard_map/buhqk,bukhd->buqhd/dot_general | solution.py:98
  205.3 2.2 copy.61
  207.5 1.6 reshape_transpose_reshape.12
  209.2 5.0 %all-to-all-start.3 = ((bf16[32,1,8,2560]{3,2,1,0:T(8,128)(2,1)}), bf16[32,1,8,2560]{3,2,1,0:T(8,128)(2,1)S(1)}, u32[]{:S(2)}, u32[]{:S(2)}) async-start(bf16[32,1,8,2560]{3,2,1,0:T(8,128)(2,1)} %bitcast.18), calls=%async_computation.3 | async-start | bytes 2621440 | tf_op jit(solution)/shard_map/all_to_all | solution.py:105
  216.4 6.1 %fusion.44 = (f32[20,256]{1,0:T(8,128)S(1)}, f32[20,256,256]{1,2,0:T(8,128)}) fusion(pred[256,256]{0,1:T(8,128)(4,1)S(1)} %select_bitcast_fusion.3, bf16[256,20,128]{0,2,1:T(8,128)(2,1)} %bitcast.77, bf16[256,20,128]{0,2,1:T(8,128)(2,1)} %bitcast.78), kind=kOutput, calls=%fused_computation.100 | convolution fusion | flops 340787456 | bytes 7950336 | tf_op jit(solution)/shard_map/sub | solution.py:15
  222.5 4.5 %fusion.17 = f32[20,256,128]{1,2,0:T(8,128)} fusion(bf16[256,20,128]{0,2,1:T(8,128)(2,1)S(1)} %bitcast.76, f32[20,256,256]{1,2,0:T(8,128)} %get-tuple-element.10, f32[20,256]{1,0:T(8,128)S(1)} %get-tuple-element.9), kind=kOutput, calls=%fused_computation.33 | convolution fusion | flops 339476480 | bytes 9195520 | tf_op jit(solution)/shard_map/hqk,khd->qhd/dot_general | solution.py:45
  227.1 3.2 copy.63
  230.4 30.1 %all-to-all-done.3 = bf16[32,1,8,2560]{3,2,1,0:T(8,128)(2,1)S(1)} async-done(((bf16[32,1,8,2560]{3,2,1,0:T(8,128)(2,1)}), bf16[32,1,8,2560]{3,2,1,0:T(8,128)(2,1)S(1)}, u32[]{:S(2)}, u32[]{:S(2)}) %all-to-all-start.3) | async-done | bytes 1310752 | tf_op jit(solution)/shard_map/all_to_all | solution.py:105
  261.1 49.9 %all-gather.3.cloned.1.call-done = bf16[2560,5120]{0,1:T(8,128)(2,1)} async-done(((bf16[2560,160]{0,1:T(8,128)(2,1)}), bf16[2560,5120]{0,1:T(8,128)(2,1)}) %all-gather.3.cloned.1.call-update) | async-done | bytes 26214416 | tf_op jit(solution)/shard_map/all_gather | solution.py:117
  311.0 14.0 %fusion.2 = bf16[1,1,256,5120]{3,2,1,0:T(8,128)(2,1)} fusion(bf16[2560,5120]{0,1:T(8,128)(2,1)} %all-gather.3.cloned.1.call-done, f32[256,2560]{1,0:T(8,128)} %copy.63, bf16[32,8,2560]{2,1,0:T(8,128)(2,1)S(1)} %gather_fusion.5, pred[32]{0:T(512)(128)(4,1)S(1)} %compare_and_fusion.1), kind=kOutput, calls=%fused_computation.9 | convolution fusion | flops 6714818560 | bytes 32768032 | tf_op jit(solution)/shard_map/dot_general | solution.py:115
  (69 shorter events, 18.0 us)
Async XLA Ops:
  6.5 304.4 %all-gather.3.cloned.1.call-start = ((), (), s32[]{:S(2)}) async-start(), calls=%async_computation.4 | async-start | bytes 27033600 | tf_op jit(solution)/shard_map/all_gather | solution.py:117
  23.9 1.6 copy-start.14
  23.9 1.7 copy-start.2
  25.5 1.7 copy-start
  27.2 1.7 copy-start.1
  133.5 51.6 %all-to-all-start.1 = ((bf16[1,32,8,2560]{3,2,0,1:T(8,128)(2,1)}), bf16[1,32,8,2560]{3,2,0,1:T(8,128)(2,1)}, u32[]{:S(2)}, u32[]{:S(2)}) async-start(bf16[1,32,8,2560]{3,2,0,1:T(8,128)(2,1)} %get-tuple-element.6), calls=%async_computation.1 | async-start | bytes 2621440 | tf_op jit(solution)/shard_map/all_to_all | solution.py:56
  139.8 1.5 copy-start.3
  141.3 1.6 copy-start.8
  147.6 1.6 copy-start.12
  147.6 1.7 copy-start.13
  147.6 1.9 copy-start.5
  150.3 1.4 copy-start.4
  154.0 33.7 %copy-start.6 = (bf16[4,1,64,20,128]{4,2,3,0,1:T(8,128)(2,1)S(1)}, bf16[4,1,64,20,128]{4,2,3,0,1:T(8,128)(2,1)}, u32[]{:S(2)}) copy-start(bf16[4,1,64,20,128]{4,2,3,0,1:T(8,128)(2,1)} %copy.58) | copy-start | bytes 3932164
  190.8 1.5 copy-start.7
  192.4 1.4 copy-start.10
  192.4 1.7 copy-start.11
  209.2 51.3 %all-to-all-start.3 = ((bf16[32,1,8,2560]{3,2,1,0:T(8,128)(2,1)}), bf16[32,1,8,2560]{3,2,1,0:T(8,128)(2,1)S(1)}, u32[]{:S(2)}, u32[]{:S(2)}) async-start(bf16[32,1,8,2560]{3,2,1,0:T(8,128)(2,1)} %bitcast.18), calls=%async_computation.3 | async-start | bytes 2621440 | tf_op jit(solution)/shard_map/all_to_all | solution.py:105
  216.4 6.1 %copy-start.9 = (bf16[1,1,256,2560]{2,3,1,0:T(8,128)(2,1)S(1)}, bf16[1,1,256,2560]{2,3,1,0:T(8,128)(2,1)}, u32[]{:S(2)}) copy-start(bf16[1,1,256,2560]{2,3,1,0:T(8,128)(2,1)} %copy.54) | copy-start | bytes 3932164
Sparse Core Ops, SparseCore 0:
  25.6 285.3 all-gather.2
where the time goes:
time: 333 us; the launch traced here: 332 us
  blocking collectives  116 us (35%)
  waiting for transfers between devices  111 us (33%)
  matrix products  39 us (12%)
  local copies, waits for them, and re-layouts  36.2 us (11%)
  between operations  13.7 us (4%)
  starting transfers between devices  9.89 us (3%)
  other arithmetic  5.68 us (2%)
    all_to_all x1, blocking collectives, shards(): lax.all_to_all(ordered_k, 'seq', split_axis=1, concat_axis=0, tiled=True)  58.4 us
    all_gather x1, waiting for transfers between devices, shards(): lax.all_gather(weight_block, 'seq', axis=1, tiled=True)  49.9 us
    all_to_all x1, blocking collectives, shards(): lax.all_to_all(ordered_v, 'seq', split_axis=1, concat_axis=0, tiled=True)  40.9 us
    all_to_all x1, waiting for transfers between devices, shards(): lax.all_to_all(ordered_q, 'seq', split_axis=1, concat_axis=0, tiled=True)  31.1 us
    all_to_all x1, waiting for transfers between devices, shards(): lax.all_to_all(temporal_out, 'seq', split_axis=0, concat_axis=1, tiled=True)  30.1 us
    all_gather x1, blocking collectives, shards(): weight_block = lax.all_gather(out_weight, 'fsdp', axis=0, tiled=True)  17 us
    dot_general x1, matrix products, shards(): jnp.dot(combined, lax.all_gather(weight_block, 'seq', axis=1, tiled=True)...  14 us
    dot_general x1, matrix products, shards(): jnp.einsum('buhqk,bukhd->buqhd', temporal_probs, joined_values, preferred...  11.2 us
  transfers between devices with their start and end apart: 3, of which 3 were waited for; matrix products, arithmetic and copies ran while one was open for 19% of the time, Pallas kernels for 0%

commit v1 on v0

v1 whole, which is shorter than its diff:
```python
import functools

import jax
import jax.numpy as jnp
from jax import lax
from jax.experimental import pallas as pl
from jax.experimental.pallas import tpu as pltpu
from jax.sharding import PartitionSpec as P

MESH = pl.DeviceIdType.MESH
HEADS = 20
HD = 128
TILE = 8
CACHE = 8
HH = 2560
D = 5120
BF16 = jnp.bfloat16
F32 = jnp.float32
NEG = -1e30
LOG2E = 1.4426950408889634
SCALE2 = HD ** (-0.5) * LOG2E
NT = (((1,), (1,)), ((), ()))


def softmax_parts(scores):
    top = jnp.max(scores, axis=-1, keepdims=True)
    weights = jnp.exp2(scores - top)
    total = jnp.sum(weights, axis=-1, keepdims=True)
    return weights.astype(BF16), 1.0 / total


def kernel(
    q_ref,
    k_ref,
    v_ref,
    perm_ref,
    back_ref,
    near_ref,
    live_ref,
    ck_ref,
    cv_ref,
    w_ref,
    out_ref,
    send,
    recv,
    cache,
    o_send,
    o_recv,
    mixed,
    pair,
    wt,
    out_buf,
    one_s,
    one_r,
    loc,
    qkv_s,
    qkv_r,
    cache_s,
    cache_r,
    o_s,
    o_r,
    z_s,
    z_r,
    y_s,
    y_r,
    x_s,
    x_r,
    m_s,
    m_r,
    out_s,
):
    s = lax.axis_index("seq")
    f = lax.axis_index("fsdp")
    z, y = s // 4, s % 4
    x, c = f // 2, f % 2
    even = (z + 1) % 2
    sigma = 1 - 2 * even
    base = (z // 2) * 2
    me = (z % 2) * 4 + y

    def at(dx=0, dy=0, dz=0):
        return (((z + dz) % 8) * 4 + (y + dy) % 4, ((x + dx) % 4) * 2 + c)

    partner = (s, x * 2 + (1 - c))

    def member(index):
        return ((base + index // 4) * 4 + index % 4, f)

    def remote(src, dst, ss, rs, device):
        return pltpu.make_async_remote_copy(
            src_ref=src, dst_ref=dst, send_sem=ss, recv_sem=rs, device_id=device, device_id_type=MESH
        )

    barrier = pltpu.get_barrier_semaphore()
    greeted = [partner, at(dx=1), at(dx=3)]
    greeted += [member((me + d) % 8) for d in range(1, 8)]
    greeted += [at(dz=sigma), at(dz=2 * sigma + 8), at(dz=3 * sigma + 8)]
    for device in greeted:
        pl.semaphore_signal(barrier, inc=1, device_id=device, device_id_type=MESH)
    pl.semaphore_wait(barrier, len(greeted))

    raw_remote = remote(w_ref, pair.at[pl.ds(c * 320, 320)], one_s.at[0], one_r.at[0], partner)
    raw_remote.start()
    raw_local = pltpu.make_async_copy(w_ref, pair.at[pl.ds(c * 320, 320)], loc.at[0])
    raw_local.start()

    for index, ref in enumerate((q_ref, k_ref, v_ref)):

        @pl.loop(0, 5)
        def _(step, index=index, ref=ref):
            cols = pl.ds(pl.multiple_of(step * 512, 512), 512)
            rows = jnp.dot(perm_ref[...], ref[:, cols], preferred_element_type=F32)
            send[:, index, :, cols] = rows.astype(BF16).reshape(8, 32, 512)

    raw_local.wait()
    raw_remote.wait()
    pick = lax.broadcasted_iota(jnp.int32, (80, 160), 1) == (
        lax.broadcasted_iota(jnp.int32, (80, 160), 0) + c * 80
    )
    chunk = lax.dot_general(
        jnp.where(pick, 1.0, 0.0).astype(BF16), pair[...], NT, preferred_element_type=F32
    )
    half = pl.ds(pl.multiple_of(c * 80, 16), 80)

    def lanes(dx):
        return pl.ds(pl.multiple_of(((x + dx) % 4) * 640, 128), 640)

    wt[z, y, half, lanes(0)] = chunk.astype(BF16)

    def zof(i):
        rel = -((i + 1) // 2) if i % 2 else i // 2
        return (z + rel + 8) % 8

    def z_move(i, step):
        ref = wt.at[zof(i), y, half, lanes(0)]
        to_right = step[0] == "r"
        slot = step[1] + (0 if to_right else 4)
        return remote(ref, ref, z_s.at[slot], z_r.at[slot], at(dz=1 if to_right else 7))

    def y_move(i, kind):
        if kind == 0:
            ref, device = wt.at[zof(i), y, half, lanes(0)], at(dy=1)
        elif kind == 1:
            ref, device = wt.at[zof(i), y, half, lanes(0)], at(dy=3)
        elif i % 2 == 0:
            ref, device = wt.at[zof(i), (y + 3) % 4, half, lanes(0)], at(dy=1)
        else:
            ref, device = wt.at[zof(i), (y + 1) % 4, half, lanes(0)], at(dy=3)
        return remote(ref, ref, y_s.at[i, kind], y_r.at[i, kind], device)

    def x_move(i, kind):
        if kind == 0:
            ref, device = wt.at[zof(i), :, half, lanes(0)], at(dx=1)
        elif kind == 1:
            ref, device = wt.at[zof(i), :, half, lanes(0)], at(dx=3)
        elif kind == 2:
            ref, device = wt.at[zof(i), pl.ds(0, 2), half, lanes(3)], at(dx=1)
        else:
            ref, device = wt.at[zof(i), pl.ds(2, 2), half, lanes(1)], at(dx=3)
        return remote(ref, ref, x_s.at[i, kind], x_r.at[i, kind], device)

    def mirror(i):
        ref = wt.at[zof(i), :, half]
        return remote(ref, ref, m_s.at[i], m_r.at[i], partner)

    z_move(0, ("r", 0)).start()
    z_move(0, ("l", 0)).start()
    y_move(0, 0).start()
    y_move(0, 1).start()

    qkv_moves = []
    for d in range(1, 8):
        to = (me + d) % 8
        qkv_moves.append(
            remote(send.at[to], recv.at[me], qkv_s.at[d], qkv_r.at[d], member(to))
        )
    cache_moves = []
    for j, off in ((1, sigma), (2, 8 - 2 * sigma), (3, 3 * sigma + 8)):
        to_z = (z + off + 8) % 8
        for n, ref in enumerate((ck_ref, cv_ref)):
            cache_moves.append(
                remote(
                    ref.at[to_z // 2], cache.at[j, n], cache_s.at[j, n], cache_r.at[j, n], (to_z * 4 + y, f)
                )
            )
    for move in qkv_moves + cache_moves:
        move.start()
    locals_ = [
        pltpu.make_async_copy(send.at[me], recv.at[me], loc.at[1]),
        pltpu.make_async_copy(ck_ref.at[z // 2], cache.at[0, 0], loc.at[2]),
        pltpu.make_async_copy(cv_ref.at[z // 2], cache.at[0, 1], loc.at[3]),
    ]
    for move in locals_:
        move.start()

    def spatial(first, count):
        @pl.loop(first, first + count)
        def _(h):
            cols = pl.ds(pl.multiple_of(h * HD, HD), HD)
            scores = lax.dot_general(q_ref[:, cols], k_ref[:, cols], NT, preferred_element_type=F32)
            weights, inverse = softmax_parts(scores * SCALE2 + near_ref[...])
            values = jnp.dot(weights, v_ref[:, cols], preferred_element_type=F32)
            mixed[:, cols] = (values * inverse).astype(BF16)

    for i in range(1, 8):
        k = (i + 1) // 2
        if i % 2:
            z_move(i, ("r", k - 1)).wait_recv()
            if k < 4:
                z_move(i, ("r", k)).start()
        else:
            z_move(i, ("l", k - 1)).wait_recv()
            if k < 3:
                z_move(i, ("l", k)).start()
        y_move(i, 0).start()
        y_move(i, 1).start()

    def y_steps(i):
        y_move(i, 0).wait_recv()
        if i % 2 == 0:
            y_move(i, 2).start()
        y_move(i, 1).wait_recv()
        if i % 2:
            y_move(i, 2).start()
        y_move(i, 2).wait_recv()
        x_move(i, 0).start()
        x_move(i, 1).start()

    def x_steps(i):
        x_move(i, 0).wait_recv()
        x_move(i, 2).start()
        x_move(i, 1).wait_recv()
        x_move(i, 3).start()

    def x_last(i):
        x_move(i, 2).wait_recv()
        x_move(i, 3).wait_recv()
        mirror(i).start()

    for i in range(8):
        y_steps(i)
        if i > 0:
            x_steps(i - 1)
        if i > 1:
            x_last(i - 2)
        if i < 5:
            spatial(i * 4, 4)

    for move in locals_:
        move.wait()
    for move in qkv_moves + cache_moves:
        move.wait_recv()

    for p in range(2):

        @pl.loop(0, HEADS)
        def _(h, p=p):
            cols = pl.ds(pl.multiple_of(h * HD, HD), HD)
            rows = pl.ds(p * 16, 16)
            slots = pl.ds(p * 2, 2)
            queries = recv[:, 0, rows, cols].reshape(128, HD)
            span_k = recv[:, 1, rows, cols].reshape(128, HD)
            span_v = recv[:, 2, rows, cols].reshape(128, HD)
            old_k = cache[slots, 0, :, cols].reshape(128, HD)
            old_v = cache[slots, 1, :, cols].reshape(128, HD)
            keys = jnp.concatenate([span_k, old_k], axis=0)
            values = jnp.concatenate([span_v, old_v], axis=0)
            scores = lax.dot_general(queries, keys, NT, preferred_element_type=F32)
            weights, inverse = softmax_parts(scores * SCALE2 + live_ref[...])
            result = jnp.dot(weights, values, preferred_element_type=F32) * inverse
            o_send[:, rows, cols] = result.astype(BF16).reshape(8, 16, HD)

    o_moves = []
    for d in range(1, 8):
        to = (me + d) % 8
        o_moves.append(remote(o_send.at[to], o_recv.at[me], o_s.at[d], o_r.at[d], member(to)))
    for move in o_moves:
        move.start()
    o_local = pltpu.make_async_copy(o_send.at[me], o_recv.at[me], loc.at[4])
    o_local.start()

    x_steps(7)
    x_last(6)

    o_local.wait()
    for move in o_moves:
        move.wait_recv()

    @pl.loop(0, 5)
    def _(step):
        cols = pl.ds(pl.multiple_of(step * 512, 512), 512)
        rows = jnp.dot(back_ref[...], o_recv[:, :, cols].reshape(256, 512), preferred_element_type=F32)
        mixed[:, cols] = (mixed[:, cols].astype(F32) + rows).astype(BF16)

    def out_move(i):
        cols = pl.ds(pl.multiple_of(zof(i) * 640, 128), 640)
        return pltpu.make_async_copy(out_buf.at[i % 2], out_ref.at[:, cols], out_s.at[i % 2])

    def project(i):
        mirror(i).wait_recv()
        if i > 1:
            out_move(i - 2).wait()
        block = wt[zof(i)].reshape(640, HH)
        result = lax.dot_general(mixed[...], block, NT, preferred_element_type=F32)
        out_buf[i % 2] = result.astype(BF16)
        out_move(i).start()

    for i in range(7):
        project(i)
    x_last(7)
    project(7)
    out_move(6).wait()
    out_move(7).wait()

    for move in qkv_moves + cache_moves + o_moves:
        move.wait_send()
    for k in range(4):
        z_move(0, ("r", k)).wait_send()
    for k in range(3):
        z_move(0, ("l", k)).wait_send()
    for i in range(8):
        for kind in range(3):
            y_move(i, kind).wait_send()
        for kind in range(4):
            x_move(i, kind).wait_send()
        mirror(i).wait_send()


def shards(queries, key_rows, value_rows, cache_keys, cache_values, cache_frames, neighbors, tile_order, out_weight):
    s = lax.axis_index("seq")
    block = s // 8
    tokens = jnp.arange(256, dtype=jnp.int32)
    index, j, tok = tokens // 32, (tokens // 8) % 4, tokens % 8
    side = index // 4
    slot = ((block * 2 + side + j * (2 * side - 1) + 8) % 8) * 4 + index % 4
    tile_ids = jnp.arange(32, dtype=jnp.int32)
    tile = jnp.sum(jnp.where(slot[:, None] == tile_ids[None, :], tile_order[None, :], 0), axis=1)
    source = tile * 8 + tok
    perm = (source[:, None] == tokens[None, :]).astype(BF16)
    back = (tokens[:, None] == source[None, :]).astype(BF16)
    near = jnp.any(neighbors[:, :, None] == tile_ids[None, None, :], axis=1)
    near = jnp.where(near, 0.0, NEG).astype(F32)
    near = jnp.broadcast_to(near[:, None, :, None], (32, 8, 32, 8)).reshape(256, 256)
    rows = jnp.arange(128, dtype=jnp.int32)
    row_frame, row_slot = rows // 16, (rows // 8) % 2
    span = (row_slot[:, None] == row_slot[None, :]) & (row_frame[None, :] <= row_frame[:, None])
    frames = jnp.sum(jnp.where(jnp.arange(4, dtype=jnp.int32) == block, cache_frames[:, 0], 0))
    old = (row_slot[:, None] == rows[None, :] // 64) & ((rows[None, :] // 8) % 8 >= CACHE - frames)
    live = jnp.where(jnp.concatenate([span, old], axis=1), 0.0, NEG).astype(F32)

    vmem = pl.BlockSpec(memory_space=pltpu.VMEM)
    hbm = pl.BlockSpec(memory_space=pl.ANY)
    dma = pltpu.SemaphoreType.DMA
    out = pl.pallas_call(
        kernel,
        out_shape=jax.ShapeDtypeStruct((256, D), BF16),
        in_specs=[vmem] * 7 + [hbm] * 3,
        out_specs=hbm,
        scratch_shapes=[
            pltpu.VMEM((8, 3, 32, HH), BF16),
            pltpu.VMEM((8, 3, 32, HH), BF16),
            pltpu.VMEM((4, 2, 64, HH), BF16),
            pltpu.VMEM((8, 32, HH), BF16),
            pltpu.VMEM((8, 32, HH), BF16),
            pltpu.VMEM((256, HH), BF16),
            pltpu.VMEM((640, 160), BF16),
            pltpu.VMEM((8, 4, 160, HH), BF16),
            pltpu.VMEM((2, 256, 640), BF16),
            dma((1,)),
            dma((1,)),
            dma((5,)),
            dma((8,)),
            dma((8,)),
            dma((4, 2)),
            dma((4, 2)),
            dma((8,)),
            dma((8,)),
            dma((8,)),
            dma((8,)),
            dma((8, 3)),
            dma((8, 3)),
            dma((8, 4)),
            dma((8, 4)),
            dma((8,)),
            dma((8,)),
            dma((2,)),
        ],
        compiler_params=pltpu.CompilerParams(
            collective_id=0, has_side_effects=True, vmem_limit_bytes=60 * 2**20
        ),
        cost_estimate=pl.CostEstimate(flops=9 * 10**9, bytes_accessed=2 * 10**7, transcendentals=3 * 10**6),
    )(
        queries.reshape(256, HH),
        key_rows.reshape(256, HH),
        value_rows.reshape(256, HH),
        perm,
        back,
        near,
        live,
        cache_keys.reshape(4, 64, HH),
        cache_values.reshape(4, 64, HH),
        out_weight,
    )
    return out.reshape(1, 1, 256, D)


def solution(mesh):
    placed = (
        P("seq", "fsdp", None, None),
        P("seq", "fsdp", None, None),
        P("seq", "fsdp", None, None),
        P("seq", None, "fsdp", None, None),
        P("seq", None, "fsdp", None, None),
        P(None, "fsdp"),
        P(),
        P(),
        P("fsdp", "seq"),
    )
    return jax.shard_map(
        shards, mesh=mesh, in_specs=placed, out_specs=P("seq", "fsdp", None, None), check_vma=False
    )
```

time: 333 us -> 271 us (0.81)
  Pallas kernels: 0 us -> 254 us
  blocking collectives: 116 us -> 0 us
  waiting for transfers between devices: 111 us -> 0 us
  matrix products: 39 us -> 0 us
  local copies, waits for them, and re-layouts: 36.2 us -> 12.3 us
  between operations: 13.7 us -> 0.7 us
  starting transfers between devices: 9.89 us -> 0 us
    pallas_call x0 -> x1, Pallas kernels: none -> 254 us  [shards(): pl.pallas_call(kernel, out_shape=jax.ShapeDtypeStruct((256, D), BF16), in...]
    all_to_all x2 -> x0, blocking collectives: 99.3 us -> none  [the longest x1 58.4 us: shards(): lax.all_to_all(ordered_k, 'seq', split_axis=1, concat_axis=0, tiled=True)]
    all_to_all x2 -> x0, waiting for transfers between devices: 61.1 us -> none  [the longest x1 31.1 us: shards(): lax.all_to_all(ordered_q, 'seq', split_axis=1, concat_axis=0, tiled=True)]
    all_gather x1 -> x0, waiting for transfers between devices: 49.9 us -> none  [shards(): lax.all_gather(weight_block, 'seq', axis=1, tiled=True)]
    dot_general x4 -> x0, matrix products: 32.9 us -> none  [the longest x1 14 us: shards(): jnp.dot(combined, lax.all_gather(weight_block, 'seq', axis=1, tiled=True)...]
    all_gather x1 -> x0, blocking collectives: 17 us -> none  [shards(): weight_block = lax.all_gather(out_weight, 'fsdp', axis=0, tiled=True)]
    another operation x10 -> x0, local copies, waits for them, and re-layouts: 14.9 us -> none  [the longest x4 4.45 us: slot_major(): return moved.reshape(groups, SPAN, slot_count, TILE, HEADS, HD).transpose...]
    all_to_all x2 -> x0, starting transfers between devices: 9.88 us -> none  [the longest x1 5.03 us: shards(): lax.all_to_all(temporal_out, 'seq', split_axis=0, concat_axis=1, tiled=True)]
  transfers between devices with their start and end apart: 3 -> 0, of which waited for: 3 -> 0; matrix products, arithmetic and copies ran while one was open for 19% -> 0% of each run, Pallas kernels for 0% -> 0%
where the time goes in v1:
time: 271 us
  Pallas kernels  254 us (94%)
  local copies, waits for them, and re-layouts  12.3 us (5%)
  other arithmetic  4.42 us (2%)
    pallas_call x1, Pallas kernels, shards(): pl.pallas_call(kernel, out_shape=jax.ShapeDtypeStruct((256, D), BF16), in...  254 us

profile of v1, /device:TPU:1, one launch (start us, length us, event | category | flops | bytes accessed | tf_op | source)
XLA Modules:
  0.0 271.2 jit_solution(10293924610460003668)
XLA Ops:
  0.0 1.3 fusion.14
  2.0 0.7 select_reduce_fusion
  2.7 0.8 fusion.2
  3.6 0.1 compare_and_fusion.1
  3.7 0.7 add_select_fusion.live_ref
  4.4 1.7 copy.14.w_ref
  6.0 0.8 fusion.1
  6.8 2.5 broadcast_in_dim.58
  9.3 4.7 %reshape.280.near_ref = f32[256,256]{1,0:T(8,128)} reshape(f32[32,8,32,8]{3,2,1,0:T(8,128)} %broadcast_in_dim.58) | data formatting | bytes 524288 | tf_op jit(solution)/shard_map/reshape | solution.py:343
  14.0 253.8 %shard_map.91 = bf16[256,5120]{1,0:T(8,128)(2,1)} custom-call(bf16[256,2560]{1,0:T(8,128)(2,1)} %bitcast.11, bf16[256,2560]{1,0:T(8,128)(2,1)} %bitcast.12, bf16[256,2560]{1,0:T(8,128)(2,1)} %bitcast.13, bf16[256,256]{1,0:T(8,128)(2,1)} %get-tuple-element.6.perm_ref, bf16[256,256]{1,0:T(8,128)(2,1)} %get-tuple-element.5.back_ref, ...), custom_call_target="tpu_custom_call" | custom-call | flops 8999999488 | bytes 20000000 | tf_op jit(solution)/shard_map/pallas_call | solution.py:354
  267.8 3.4 %copy.16 = bf16[1,1,256,5120]{3,2,1,0:T(8,128)(2,1)} copy(bf16[1,1,256,5120]{3,2,1,0:T(8,128)(2,1)} %bitcast.10) | data formatting | bytes 5242880
  (6 shorter events, 0.1 us)

commit v2 on v1

v2 whole, which is shorter than its diff:
```python
import functools

import jax
import jax.numpy as jnp
from jax import lax
from jax.experimental import pallas as pl
from jax.experimental.pallas import tpu as pltpu
from jax.sharding import PartitionSpec as P

MESH = pl.DeviceIdType.MESH
HEADS = 20
HD = 128
TILE = 8
CACHE = 8
HH = 2560
HALF = 1280
TEMPORAL_UNROLL = 5
SCHEDULE = ('k1', 'z1', 'z2', 'y0', 'z3', 'z4', 'y1', 'z5', 'z6', 'y2', 'z7', 'a0', 'a1', 's0', 'x0', 'l0', 'y3', 's1', 'x1', 'l1', 'y4', 's2', 'y5', 's3', 'x2', 'l2', 's4', 'y6', 'y7', 't0', 'x3', 'l3', 'x4', 'l4', 'c0', 'p0', 'p1', 'p2', 'p3', 'x5', 'l5', 'p4', 't1', 'x6', 'l6', 'p5', 'c1', 'p10', 'p11', 'p12', 'x7', 'p13', 'p14', 'p15', 'p6', 'p16', 'l7', 'p7', 'p17')
D = 5120
BF16 = jnp.bfloat16
F32 = jnp.float32
NEG = -1e30
LOG2E = 1.4426950408889634
SCALE2 = HD ** (-0.5) * LOG2E
NT = (((1,), (1,)), ((), ()))


def softmax_parts(scores):
    top = jnp.max(scores, axis=-1, keepdims=True)
    weights = jnp.exp2(scores - top)
    total = jnp.sum(weights, axis=-1, keepdims=True)
    return weights.astype(BF16), 1.0 / total


def tables(z, order_ref, near_tiles_ref, frames_ref, perm_ref, back_ref, near_ref, live_ref):
    def iota(shape, dim):
        return lax.broadcasted_iota(jnp.int32, shape, dim)

    def slot_of(token):
        index, j = token // 32, (token // 8) % 4
        side = index // 4
        return (((z // 2) * 2 + side + j * (2 * side - 1) + 8) % 8) * 4 + index % 4

    order = order_ref[...]
    held = iota((256, 32), 1) == slot_of(iota((256, 32), 0))
    tile = jnp.sum(jnp.where(held, jnp.broadcast_to(order, (256, 32)), 0), axis=1, keepdims=True)
    source = tile * 8 + iota((256, 1), 0) % 8
    perm_ref[...] = jnp.where(source == iota((256, 256), 1), 1.0, 0.0).astype(BF16)
    held = iota((32, 256), 0) == slot_of(iota((32, 256), 1))
    tile = jnp.dot(
        jnp.broadcast_to(order, (8, 32)).astype(F32).astype(BF16),
        jnp.where(held, 1.0, 0.0).astype(BF16),
        preferred_element_type=F32,
    )[:1].astype(jnp.int32)
    source = tile * 8 + iota((1, 256), 1) % 8
    back_ref[...] = jnp.where(source == iota((256, 256), 0), 1.0, 0.0).astype(BF16)

    mine = iota((256, 32), 1) == iota((256, 32), 0) // 8
    tiles = lax.dot_general(
        jnp.where(mine, 1.0, 0.0).astype(BF16),
        near_tiles_ref[...].astype(F32).astype(BF16),
        NT,
        preferred_element_type=F32,
    ).astype(jnp.int32)
    column = iota((256, 256), 1) // 8
    near = tiles[:, 0:1] == column
    for n in range(1, 9):
        near = near | (tiles[:, n : n + 1] == column)
    near_ref[...] = jnp.where(near, 0.0, NEG)

    row, col = iota((128, 256), 0), iota((128, 256), 1)
    span = (col < 128) & ((row // 8) % 2 == (col // 8) % 2) & (col // 16 <= row // 16)
    old = (col >= 128) & ((row // 8) % 2 == (col - 128) // 64)
    old = old & ((col // 8) % 8 >= CACHE - frames_ref[0, z // 2])
    live_ref[...] = jnp.where(span | old, 0.0, NEG)


def kernel(
    q_hbm,
    k_hbm,
    v_hbm,
    order_ref,
    near_tiles_ref,
    frames_ref,
    ck_ref,
    cv_ref,
    w_ref,
    out_ref,
    send,
    recv,
    cache,
    o_send,
    o_recv,
    mixed,
    q_ref,
    k_ref,
    v_ref,
    perm_ref,
    back_ref,
    near_ref,
    live_ref,
    pair,
    wt,
    out_buf,
    total,
    one_s,
    one_r,
    loc,
    qkv_s,
    qkv_r,
    cache_s,
    cache_r,
    o_s,
    o_r,
    z_s,
    z_r,
    y_s,
    y_r,
    x_s,
    x_r,
    f_s,
    f_r,
    m_s,
    m_r,
    out_s,
):
    s = lax.axis_index("seq")
    f = lax.axis_index("fsdp")
    z, y = s // 4, s % 4
    x, c = f // 2, f % 2
    even = (z + 1) % 2
    sigma = 1 - 2 * even
    base = (z // 2) * 2
    me = (z % 2) * 4 + y

    def at(dx=0, dy=0, dz=0):
        return (((z + dz) % 8) * 4 + (y + dy) % 4, ((x + dx) % 4) * 2 + c)

    partner = (s, x * 2 + (1 - c))

    def member(index):
        return ((base + index // 4) * 4 + index % 4, f)

    def remote(src, dst, ss, rs, device):
        return pltpu.make_async_remote_copy(
            src_ref=src, dst_ref=dst, send_sem=ss, recv_sem=rs, device_id=device, device_id_type=MESH
        )

    half = pl.ds(pl.multiple_of(c * 80, 16), 80)
    barrier = pltpu.get_barrier_semaphore()
    greeted = [partner, at(dx=1), at(dx=3)]
    greeted += [member((me + d) % 8) for d in range(1, 8)]
    greeted += [at(dz=sigma), at(dz=2 * sigma + 8), at(dz=3 * sigma + 8)]
    for device in greeted:
        pl.semaphore_signal(barrier, inc=1, device_id=device, device_id_type=MESH)
    staged = [
        pltpu.make_async_copy(src, dst, loc.at[1, n])
        for n, (src, dst) in enumerate(((q_hbm, q_ref), (k_hbm, k_ref), (v_hbm, v_ref)))
    ]
    for move in staged:
        move.start()
    raw_local = pltpu.make_async_copy(w_ref.at[half], pair.at[c], loc.at[0, 0])
    raw_local.start()
    pl.semaphore_wait(barrier, len(greeted))

    other = pl.ds(pl.multiple_of((1 - c) * 80, 16), 80)
    raw_remote = remote(w_ref.at[other], pair.at[c], one_s.at[0], one_r.at[0], partner)
    raw_remote.start()
    def pack(h):
        for index, ref in enumerate((q_ref, k_ref, v_ref)):

            @pl.loop(0, 5)
            def _(step, index=index, ref=ref):
                cols = pl.ds(pl.multiple_of(step * 256, 256), 256)
                from_cols = pl.ds(pl.multiple_of(h * HALF + step * 256, 256), 256)
                rows = jnp.dot(perm_ref[...], ref[:, from_cols], preferred_element_type=F32)
                send[h, :, index, :, cols] = rows.astype(BF16).reshape(8, 32, 256)

    raw_local.wait()
    raw_remote.wait()
    chunk = jnp.concatenate([pair[0].astype(F32), pair[1].astype(F32)], axis=1)

    def lanes(dx):
        return pl.ds(pl.multiple_of(((x + dx) % 4) * 640, 128), 640)

    wt[z, y, half, lanes(0)] = chunk.astype(BF16)

    def zof(i):
        rel = -((i + 1) // 2) if i % 2 else i // 2
        return (z + rel + 8) % 8

    def z_move(i, step):
        ref = wt.at[zof(i), y, half, lanes(0)]
        to_right = step[0] == "r"
        slot = step[1] + (0 if to_right else 4)
        return remote(ref, ref, z_s.at[slot], z_r.at[slot], at(dz=1 if to_right else 7))

    def y_move(i, kind):
        if kind == 0:
            ref, device = wt.at[zof(i), y, half, lanes(0)], at(dy=1)
        elif kind == 1:
            ref, device = wt.at[zof(i), y, half, lanes(0)], at(dy=3)
        else:
            ref, device = wt.at[zof(i), y, half, lanes(0)], at(dy=2)
        return remote(ref, ref, y_s.at[i, kind], y_r.at[i, kind], device)

    def x_move(i, kind):
        if kind == 0:
            ref, device = wt.at[zof(i), :, half, lanes(0)], at(dx=1)
        elif kind == 1:
            ref, device = wt.at[zof(i), :, half, lanes(0)], at(dx=3)
        elif kind == 2:
            ref, device = wt.at[zof(i), pl.ds(0, 2), half, lanes(3)], at(dx=1)
        else:
            ref, device = wt.at[zof(i), pl.ds(2, 2), half, lanes(1)], at(dx=3)
        return remote(ref, ref, x_s.at[i, kind], x_r.at[i, kind], device)

    def x_first(r, kind):
        row = (y + r) % 4
        if kind < 2:
            ref, device = wt.at[z, row, half, lanes(0)], at(dx=3 if kind else 1)
        elif r < 2:
            ref, device = wt.at[z, row, half, lanes(3)], at(dx=1)
        else:
            ref, device = wt.at[z, row, half, lanes(1)], at(dx=3)
        return remote(ref, ref, f_s.at[r, kind], f_r.at[r, kind], device)

    def last_mirror(n):
        rows = pl.ds(0, 2) if n == 3 else pl.ds(2, 2) if n == 4 else pl.ds(0, 4)
        ref = wt.at[zof(7), rows, half, lanes((0, 3, 1, 2, 2)[n])]
        return remote(ref, ref, m_s.at[7 + n], m_r.at[7 + n], partner)

    def mirror(i):
        ref = wt.at[zof(i), :, half]
        return remote(ref, ref, m_s.at[i], m_r.at[i], partner)

    x_first(0, 0).start()
    x_first(0, 1).start()
    z_move(0, ("r", 0)).start()
    z_move(0, ("l", 0)).start()
    for kind in range(3):
        y_move(0, kind).start()
    for move in staged:
        move.wait()
    tables(z, order_ref, near_tiles_ref, frames_ref, perm_ref, back_ref, near_ref, live_ref)
    pack(0)

    def exchange(h):
        moves = []
        lane_half = pl.ds(h * HALF, HALF)
        for j, off in ((1, sigma), (2, 8 - 2 * sigma), (3, 3 * sigma + 8)):
            to_z = (z + off + 8) % 8
            for n, ref in enumerate((ck_ref, cv_ref)):
                src = ref.at[to_z // 2, :, lane_half]
                sems = cache_s.at[h, j, n], cache_r.at[h, j, n]
                moves.append(remote(src, cache.at[h, j, n], *sems, (to_z * 4 + y, f)))
        for d in range(1, 8):
            to = (me + d) % 8
            sems = qkv_s.at[h, d], qkv_r.at[h, d]
            moves.append(remote(send.at[h, to], recv.at[h, me], *sems, member(to)))
        own = [pltpu.make_async_copy(send.at[h, me], recv.at[h, me], loc.at[h, 1])]
        for n, ref in enumerate((ck_ref, cv_ref)):
            src = ref.at[z // 2, :, lane_half]
            own.append(pltpu.make_async_copy(src, cache.at[h, 0, n], loc.at[h, 2 + n]))
        return moves, own

    exchanges = [exchange(0), exchange(1)]

    def start_exchange(h):
        for move in exchanges[h][0] + exchanges[h][1]:
            move.start()

    def spatial(first, count):
        @pl.loop(first, first + count)
        def _(h):
            cols = pl.ds(pl.multiple_of(h * HD, HD), HD)
            scores = lax.dot_general(q_ref[:, cols], k_ref[:, cols], NT, preferred_element_type=F32)
            weights, inverse = softmax_parts(scores * SCALE2 + near_ref[...])
            values = jnp.dot(weights, v_ref[:, cols], preferred_element_type=F32)
            mixed[:, cols] = (values * inverse).astype(BF16)

    def z_steps(i):
        k = (i + 1) // 2
        if i % 2:
            z_move(i, ("r", k - 1)).wait_recv()
            if k < 4:
                z_move(i, ("r", k)).start()
        else:
            z_move(i, ("l", k - 1)).wait_recv()
            if k < 3:
                z_move(i, ("l", k)).start()
        y_move(i, 0).start()
        y_move(i, 1).start()
        y_move(i, 2).start()

    def y_steps(i):
        for kind, r in enumerate((3, 1, 2)):
            y_move(i, kind).wait_recv()
            if i == 0:
                x_first(r, 0).start()
                x_first(r, 1).start()
        if i:
            x_move(i, 0).start()
            x_move(i, 1).start()

    def x_steps(i):
        if i == 0:
            for r in (0, 3, 1, 2):
                x_first(r, 0).wait_recv()
                if r < 2:
                    x_first(r, 2).start()
                x_first(r, 1).wait_recv()
                if r >= 2:
                    x_first(r, 2).start()
            return
        x_move(i, 0).wait_recv()
        x_move(i, 2).start()
        if i == 7:
            last_mirror(1).start()
        x_move(i, 1).wait_recv()
        x_move(i, 3).start()
        if i == 7:
            last_mirror(2).start()

    def x_last(i):
        if i == 0:
            for r in range(4):
                x_first(r, 2).wait_recv()
        elif i == 7:
            last_mirror(0).start()
            x_move(i, 2).wait_recv()
            last_mirror(3).start()
            x_move(i, 3).wait_recv()
            last_mirror(4).start()
            return
        else:
            x_move(i, 2).wait_recv()
            x_move(i, 3).wait_recv()
        mirror(i).start()

    def o_exchange(h):
        moves = []
        for d in range(1, 8):
            to = (me + d) % 8
            sems = o_s.at[h, d], o_r.at[h, d]
            moves.append(remote(o_send.at[h, to], o_recv.at[h, me], *sems, member(to)))
        return moves, pltpu.make_async_copy(o_send.at[h, me], o_recv.at[h, me], loc.at[h, 4])

    o_exchanges = [o_exchange(0), o_exchange(1)]

    def temporal(h):
        moves, own = exchanges[h]
        for move in own:
            move.wait()
        for move in moves:
            move.wait_recv()

        for p in range(2):
            rows = pl.ds(p * 16, 16)
            slots = pl.ds(p * 2, 2)

            def head(cols):
                queries = recv[h, :, 0, rows, cols].reshape(128, HD)
                span_k = recv[h, :, 1, rows, cols].reshape(128, HD)
                span_v = recv[h, :, 2, rows, cols].reshape(128, HD)
                old_k = cache[h, slots, 0, :, cols].reshape(128, HD)
                old_v = cache[h, slots, 1, :, cols].reshape(128, HD)
                keys = jnp.concatenate([span_k, old_k], axis=0)
                values = jnp.concatenate([span_v, old_v], axis=0)
                scores = lax.dot_general(queries, keys, NT, preferred_element_type=F32)
                weights, inverse = softmax_parts(scores * SCALE2 + live_ref[...])
                result = jnp.dot(weights, values, preferred_element_type=F32) * inverse
                o_send[h, :, rows, cols] = result.astype(BF16).reshape(8, 16, HD)

            @pl.loop(0, 10 // TEMPORAL_UNROLL)
            def _(step, head=head):
                for n in range(TEMPORAL_UNROLL):
                    head(pl.ds(pl.multiple_of((step * TEMPORAL_UNROLL + n) * HD, HD), HD))

        moves, own = o_exchanges[h]
        for move in moves:
            move.start()
        own.start()

    def combine(h):
        moves, own = o_exchanges[h]
        own.wait()
        for move in moves:
            move.wait_recv()

        @pl.loop(0, 5)
        def _(step):
            cols = pl.ds(pl.multiple_of(step * 256, 256), 256)
            to_cols = pl.ds(pl.multiple_of(h * HALF + step * 256, 256), 256)
            rows = jnp.dot(
                back_ref[...], o_recv[h, :, :, cols].reshape(256, 256), preferred_element_type=F32
            )
            mixed[:, to_cols] = (mixed[:, to_cols].astype(F32) + rows).astype(BF16)

    def out_move(i):
        cols = pl.ds(pl.multiple_of(zof(i) * 640, 128), 640)
        return pltpu.make_async_copy(out_buf.at[i % 2], out_ref.at[:, cols], out_s.at[i % 2])

    def project(i, h):
        lane_half = pl.ds(h * HALF, HALF)
        if h == 0 and i < 7:
            mirror(i).wait_recv()
        elif h == 0:
            for n in range(5):
                last_mirror(n).wait_recv()
        block = wt[zof(i), :, :, lane_half].reshape(640, HALF)
        result = lax.dot_general(mixed[:, lane_half], block, NT, preferred_element_type=F32)
        if h == 0:
            total[i] = result
        else:
            if i > 1:
                out_move(i - 2).wait()
            out_buf[i % 2] = (result + total[i]).astype(BF16)
            out_move(i).start()

    def run(step):
        kind, index = step[0], int(step[1:])
        if kind == "z":
            z_steps(index)
        elif kind == "y":
            y_steps(index)
        elif kind == "x":
            x_steps(index)
        elif kind == "l":
            x_last(index)
        elif kind == "s":
            spatial(index * 4, 4)
        elif kind == "k":
            pack(index)
        elif kind == "a":
            start_exchange(index)
        elif kind == "t":
            temporal(index)
        elif kind == "c":
            combine(index)
        elif kind == "p":
            project(index % 10, index // 10)

    for step in SCHEDULE:
        run(step)
    out_move(6).wait()
    out_move(7).wait()

    for h in range(2):
        for move in exchanges[h][0] + o_exchanges[h][0]:
            move.wait_send()
    for k in range(4):
        z_move(0, ("r", k)).wait_send()
    for k in range(3):
        z_move(0, ("l", k)).wait_send()
    for i in range(8):
        for kind in range(3):
            y_move(i, kind).wait_send()
        for kind in range(4 if i else 0):
            x_move(i, kind).wait_send()
        if i < 7:
            mirror(i).wait_send()
    for r in range(4):
        for kind in range(3):
            x_first(r, kind).wait_send()
    for n in range(5):
        last_mirror(n).wait_send()


def shards(queries, key_rows, value_rows, cache_keys, cache_values, cache_frames, neighbors, tile_order, out_weight):
    vmem = pl.BlockSpec(memory_space=pltpu.VMEM)
    hbm = pl.BlockSpec(memory_space=pl.ANY)
    dma = pltpu.SemaphoreType.DMA
    out = pl.pallas_call(
        kernel,
        out_shape=jax.ShapeDtypeStruct((256, D), BF16),
        in_specs=[hbm] * 3 + [vmem] * 2 + [pl.BlockSpec(memory_space=pltpu.SMEM)] + [hbm] * 3,
        out_specs=hbm,
        scratch_shapes=[
            pltpu.VMEM((2, 8, 3, 32, HALF), BF16),
            pltpu.VMEM((2, 8, 3, 32, HALF), BF16),
            pltpu.VMEM((2, 4, 2, 64, HALF), BF16),
            pltpu.VMEM((2, 8, 32, HALF), BF16),
            pltpu.VMEM((2, 8, 32, HALF), BF16),
            pltpu.VMEM((256, HH), BF16),
            pltpu.VMEM((256, HH), BF16),
            pltpu.VMEM((256, HH), BF16),
            pltpu.VMEM((256, HH), BF16),
            pltpu.VMEM((256, 256), BF16),
            pltpu.VMEM((256, 256), BF16),
            pltpu.VMEM((256, 256), F32),
            pltpu.VMEM((128, 256), F32),
            pltpu.VMEM((2, 80, 320), BF16),
            pltpu.VMEM((8, 4, 160, HH), BF16),
            pltpu.VMEM((2, 256, 640), BF16),
            pltpu.VMEM((8, 256, 640), F32),
            dma((1,)),
            dma((1,)),
            dma((2, 5)),
            dma((2, 8)),
            dma((2, 8)),
            dma((2, 4, 2)),
            dma((2, 4, 2)),
            dma((2, 8)),
            dma((2, 8)),
            dma((8,)),
            dma((8,)),
            dma((8, 3)),
            dma((8, 3)),
            dma((8, 4)),
            dma((8, 4)),
            dma((4, 3)),
            dma((4, 3)),
            dma((12,)),
            dma((12,)),
            dma((2,)),
        ],
        compiler_params=pltpu.CompilerParams(
            collective_id=0, has_side_effects=True, vmem_limit_bytes=60 * 2**20
        ),
        cost_estimate=pl.CostEstimate(flops=9 * 10**9, bytes_accessed=2 * 10**7, transcendentals=3 * 10**6),
    )(
        queries.reshape(256, HH),
        key_rows.reshape(256, HH),
        value_rows.reshape(256, HH),
        tile_order.reshape(1, 32),
        neighbors.T,
        cache_frames.T,
        cache_keys.reshape(4, 64, HH),
        cache_values.reshape(4, 64, HH),
        out_weight.T,
    )
    return out.reshape(1, 1, 256, D)


def solution(mesh):
    placed = (
        P("seq", "fsdp", None, None),
        P("seq", "fsdp", None, None),
        P("seq", "fsdp", None, None),
        P("seq", None, "fsdp", None, None),
        P("seq", None, "fsdp", None, None),
        P(None, "fsdp"),
        P(),
        P(),
        P("fsdp", "seq"),
    )
    return jax.shard_map(
        shards, mesh=mesh, in_specs=placed, out_specs=P("seq", "fsdp", None, None), check_vma=False
    )
```

time: 271 us -> 159 us (0.59)
  Pallas kernels: 254 us -> 155 us
  local copies, waits for them, and re-layouts: 12.3 us -> 3.4 us
  other arithmetic: 4.42 us -> 0 us
    pallas_call x1, Pallas kernels: 254 us -> 155 us  [shards(): pl.pallas_call(kernel, out_shape=jax.ShapeDtypeStruct((256, D), BF16), in...]
    reshape x1 -> x0, local copies, waits for them, and re-layouts: 4.68 us -> none  [shards(): jnp.broadcast_to(near[:, None, :, None], (32, 8, 32, 8)).reshape(256, 256)]
where the time goes in v2:
time: 159 us
  Pallas kernels  155 us (97%)
  local copies, waits for them, and re-layouts  3.4 us (2%)
    pallas_call x1, Pallas kernels, shards(): pl.pallas_call(kernel, out_shape=jax.ShapeDtypeStruct((256, D), BF16), in...  155 us
    unnamed x1, local copies, waits for them, and re-layouts  3.4 us

profile of v2, /device:TPU:1, one launch (start us, length us, event | category | flops | bytes accessed | tf_op | source)
XLA Modules:
  0.0 158.9 jit_solution(5605537002176736649)
XLA Ops:
  0.0 155.4 %shard_map.91 = bf16[256,5120]{1,0:T(8,128)(2,1)} custom-call(bf16[256,2560]{1,0:T(8,128)(2,1)} %bitcast.11, bf16[256,2560]{1,0:T(8,128)(2,1)} %bitcast.12, bf16[256,2560]{1,0:T(8,128)(2,1)} %bitcast.13, s32[1,32]{1,0:T(1,128)} %bitcast.18, s32[9,32]{1,0:T(8,128)} %bitcast.17, s32[1,4]{1,0:T(1,128)} %bitcast.19, bf16[4,64,2560]{2,1,0:T(8,128)(2,1)} %bitcast.14, ...), custom_call_target="tpu_custom_call" | custom-call | flops 8999999488 | bytes 20000000 | tf_op jit(solution)/shard_map/pallas_call | solution.py:474
  155.5 3.4 %copy.11 = bf16[1,1,256,5120]{3,2,1,0:T(8,128)(2,1)} copy(bf16[1,1,256,5120]{3,2,1,0:T(8,128)(2,1)} %bitcast.10) | data formatting | bytes 5242880

commit v3 on v2

--- a/solution.py
+++ b/solution.py
@@ -15,7 +15,7 @@
 HH = 2560
 HALF = 1280
 TEMPORAL_UNROLL = 5
-SCHEDULE = ('k1', 'z1', 'z2', 'y0', 'z3', 'z4', 'y1', 'z5', 'z6', 'y2', 'z7', 'a0', 'a1', 's0', 'x0', 'l0', 'y3', 's1', 'x1', 'l1', 'y4', 's2', 'y5', 's3', 'x2', 'l2', 's4', 'y6', 'y7', 't0', 'x3', 'l3', 'x4', 'l4', 'c0', 'p0', 'p1', 'p2', 'p3', 'x5', 'l5', 'p4', 't1', 'x6', 'l6', 'p5', 'c1', 'p10', 'p11', 'p12', 'x7', 'p13', 'p14', 'p15', 'p6', 'p16', 'l7', 'p7', 'p17')
+SCHEDULE = ('z1', 'z2', 'y0', 'b0', 'z3', 'z4', 'y1', 'k0', 'z5', 'z6', 'y2', 'z7', 'a0', 'x0', 'k1', 's0', 'y3', 's1', 'y4', 's2', 'y5', 's3', 'y6', 's4', 'y7', 'a1', 't0', 'x1', 'x2', 'x3', 'x4', 'x5', 'x6', 'x7', 'l0', 'l1', 'l2', 'l3', 'l4', 'l5', 't1', 'l6', 'c0', 'p0', 'p1', 'p2', 'p3', 'p4', 'p5', 'p6', 'c1', 'p10', 'p11', 'p12', 'p13', 'p14', 'p15', 'p16', 'l7', 'p7', 'p17')
 D = 5120
 BF16 = jnp.bfloat16
 F32 = jnp.float32
@@ -37,14 +37,14 @@
         return lax.broadcasted_iota(jnp.int32, shape, dim)
 
     def slot_of(token):
-        index, j = token // 32, (token // 8) % 4
-        side = index // 4
-        return (((z // 2) * 2 + side + j * (2 * side - 1) + 8) % 8) * 4 + index % 4
+        index, j = token >> 5, (token >> 3) & 3
+        side = index >> 2
+        return ((((z // 2) * 2 + side + j * (2 * side - 1) + 8) & 7) << 2) + (index & 3)
 
     order = order_ref[...]
     held = iota((256, 32), 1) == slot_of(iota((256, 32), 0))
     tile = jnp.sum(jnp.where(held, jnp.broadcast_to(order, (256, 32)), 0), axis=1, keepdims=True)
-    source = tile * 8 + iota((256, 1), 0) % 8
+    source = tile * 8 + (iota((256, 1), 0) & 7)
     perm_ref[...] = jnp.where(source == iota((256, 256), 1), 1.0, 0.0).astype(BF16)
     held = iota((32, 256), 0) == slot_of(iota((32, 256), 1))
     tile = jnp.dot(
@@ -52,26 +52,27 @@
         jnp.where(held, 1.0, 0.0).astype(BF16),
         preferred_element_type=F32,
     )[:1].astype(jnp.int32)
-    source = tile * 8 + iota((1, 256), 1) % 8
+    source = tile * 8 + (iota((1, 256), 1) & 7)
     back_ref[...] = jnp.where(source == iota((256, 256), 0), 1.0, 0.0).astype(BF16)
 
-    mine = iota((256, 32), 1) == iota((256, 32), 0) // 8
+    mine = iota((256, 32), 1) == iota((256, 32), 0) >> 3
     tiles = lax.dot_general(
         jnp.where(mine, 1.0, 0.0).astype(BF16),
         near_tiles_ref[...].astype(F32).astype(BF16),
         NT,
         preferred_element_type=F32,
     ).astype(jnp.int32)
-    column = iota((256, 256), 1) // 8
+    column = iota((256, 256), 1) >> 3
     near = tiles[:, 0:1] == column
     for n in range(1, 9):
         near = near | (tiles[:, n : n + 1] == column)
     near_ref[...] = jnp.where(near, 0.0, NEG)
 
     row, col = iota((128, 256), 0), iota((128, 256), 1)
-    span = (col < 128) & ((row // 8) % 2 == (col // 8) % 2) & (col // 16 <= row // 16)
-    old = (col >= 128) & ((row // 8) % 2 == (col - 128) // 64)
-    old = old & ((col // 8) % 8 >= CACHE - frames_ref[0, z // 2])
+    side = (row >> 3) & 1
+    span = (col < 128) & (side == (col >> 3) & 1) & (col >> 4 <= row >> 4)
+    old = (col >= 128) & (side == (col >> 6) & 1)
+    old = old & ((col >> 3) & 7 >= CACHE - frames_ref[0, z // 2])
     live_ref[...] = jnp.where(span | old, 0.0, NEG)
 
 
@@ -169,10 +170,9 @@
     def pack(h):
         for index, ref in enumerate((q_ref, k_ref, v_ref)):
 
-            @pl.loop(0, 5)
-            def _(step, index=index, ref=ref):
-                cols = pl.ds(pl.multiple_of(step * 256, 256), 256)
-                from_cols = pl.ds(pl.multiple_of(h * HALF + step * 256, 256), 256)
+            for step in range(5):
+                cols = pl.ds(step * 256, 256)
+                from_cols = pl.ds(h * HALF + step * 256, 256)
                 rows = jnp.dot(perm_ref[...], ref[:, from_cols], preferred_element_type=F32)
                 send[h, :, index, :, cols] = rows.astype(BF16).reshape(8, 32, 256)
 
@@ -240,11 +240,6 @@
     z_move(0, ("l", 0)).start()
     for kind in range(3):
         y_move(0, kind).start()
-    for move in staged:
-        move.wait()
-    tables(z, order_ref, near_tiles_ref, frames_ref, perm_ref, back_ref, near_ref, live_ref)
-    pack(0)
-
     def exchange(h):
         moves = []
         lane_half = pl.ds(h * HALF, HALF)
@@ -267,6 +262,9 @@
     exchanges = [exchange(0), exchange(1)]
 
     def start_exchange(h):
+        if h:
+            for move in exchanges[0][0]:
+                move.wait_send()
         for move in exchanges[h][0] + exchanges[h][1]:
             move.start()
 
@@ -388,10 +386,9 @@
         for move in moves:
             move.wait_recv()
 
-        @pl.loop(0, 5)
-        def _(step):
-            cols = pl.ds(pl.multiple_of(step * 256, 256), 256)
-            to_cols = pl.ds(pl.multiple_of(h * HALF + step * 256, 256), 256)
+        for step in range(5):
+            cols = pl.ds(step * 256, 256)
+            to_cols = pl.ds(h * HALF + step * 256, 256)
             rows = jnp.dot(
                 back_ref[...], o_recv[h, :, :, cols].reshape(256, 256), preferred_element_type=F32
             )
@@ -420,7 +417,13 @@
 
     def run(step):
         kind, index = step[0], int(step[1:])
-        if kind == "z":
+        if kind == "b":
+            for move in staged:
+                move.wait()
+            tables(
+                z, order_ref, near_tiles_ref, frames_ref, perm_ref, back_ref, near_ref, live_ref
+            )
+        elif kind == "z":
             z_steps(index)
         elif kind == "y":
             y_steps(index)
@@ -447,7 +450,7 @@
     out_move(7).wait()
 
     for h in range(2):
-        for move in exchanges[h][0] + o_exchanges[h][0]:
+        for move in (exchanges[h][0] if h else []) + o_exchanges[h][0]:
             move.wait_send()
     for k in range(4):
         z_move(0, ("r", k)).wait_send()

time: 159 us -> 144 us (0.906)
  Pallas kernels: 155 us -> 140 us
    pallas_call x1, Pallas kernels: 155 us -> 140 us  [shards(): pl.pallas_call(kernel, out_shape=jax.ShapeDtypeStruct((256, D), BF16), in...]
where the time goes in v3:
time: 144 us
  Pallas kernels  140 us (97%)
  local copies, waits for them, and re-layouts  3.4 us (2%)
    pallas_call x1, Pallas kernels, shards(): pl.pallas_call(kernel, out_shape=jax.ShapeDtypeStruct((256, D), BF16), in...  140 us
    unnamed x1, local copies, waits for them, and re-layouts  3.4 us

profile of v3, /device:TPU:1, one launch (start us, length us, event | category | flops | bytes accessed | tf_op | source)
XLA Modules:
  0.0 143.8 jit_solution(8327184480929667539)
XLA Ops:
  0.0 140.4 %shard_map.91 = bf16[256,5120]{1,0:T(8,128)(2,1)} custom-call(bf16[256,2560]{1,0:T(8,128)(2,1)} %bitcast.11, bf16[256,2560]{1,0:T(8,128)(2,1)} %bitcast.12, bf16[256,2560]{1,0:T(8,128)(2,1)} %bitcast.13, s32[1,32]{1,0:T(1,128)} %bitcast.18, s32[9,32]{1,0:T(8,128)} %bitcast.17, s32[1,4]{1,0:T(1,128)} %bitcast.19, bf16[4,64,2560]{2,1,0:T(8,128)(2,1)} %bitcast.14, ...), custom_call_target="tpu_custom_call" | custom-call | flops 8999999488 | bytes 20000000 | tf_op jit(solution)/shard_map/pallas_call | solution.py:477
  140.4 3.4 %copy.11 = bf16[1,1,256,5120]{3,2,1,0:T(8,128)(2,1)} copy(bf16[1,1,256,5120]{3,2,1,0:T(8,128)(2,1)} %bitcast.10) | data formatting | bytes 5242880

commit v4 on v3

--- a/solution.py
+++ b/solution.py
@@ -15,7 +15,7 @@
 HH = 2560
 HALF = 1280
 TEMPORAL_UNROLL = 5
-SCHEDULE = ('z1', 'z2', 'y0', 'b0', 'z3', 'z4', 'y1', 'k0', 'z5', 'z6', 'y2', 'z7', 'a0', 'x0', 'k1', 's0', 'y3', 's1', 'y4', 's2', 'y5', 's3', 'y6', 's4', 'y7', 'a1', 't0', 'x1', 'x2', 'x3', 'x4', 'x5', 'x6', 'x7', 'l0', 'l1', 'l2', 'l3', 'l4', 'l5', 't1', 'l6', 'c0', 'p0', 'p1', 'p2', 'p3', 'p4', 'p5', 'p6', 'c1', 'p10', 'p11', 'p12', 'p13', 'p14', 'p15', 'p16', 'l7', 'p7', 'p17')
+SCHEDULE = ('z1', 'z2', 'y0', 'b0', 'z3', 'z4', 'y1', 'k0', 'z5', 'z6', 'y2', 'z7', 'a0', 'x0', 'k1', 's0', 'y3', 's1', 'y7', 'y4', 's2', 'x1', 'y5', 's3', 'y6', 's4', 'x2', 'a1', 't0', 'x3', 'x4', 'x5', 'x7', 'x6', 'l0', 'l1', 'l2', 'l3', 'l7', 'l4', 'l5', 't1', 'l6', 'c0', 'p0', 'p1', 'p2', 'p3', 'p4', 'p5', 'p7', 'p6', 'c1', 'p10', 'p11', 'p12', 'p13', 'p14', 'p15', 'p17', 'p16')
 D = 5120
 BF16 = jnp.bfloat16
 F32 = jnp.float32
@@ -149,7 +149,7 @@
 
     half = pl.ds(pl.multiple_of(c * 80, 16), 80)
     barrier = pltpu.get_barrier_semaphore()
-    greeted = [partner, at(dx=1), at(dx=3)]
+    greeted = [partner, at(dx=1), at(dx=2), at(dx=3)]
     greeted += [member((me + d) % 8) for d in range(1, 8)]
     greeted += [at(dz=sigma), at(dz=2 * sigma + 8), at(dz=3 * sigma + 8)]
     for device in greeted:
@@ -196,7 +196,9 @@
         return remote(ref, ref, z_s.at[slot], z_r.at[slot], at(dz=1 if to_right else 7))
 
     def y_move(i, kind):
-        if kind == 0:
+        if i == 7:
+            ref, device = wt.at[zof(i), y, half, lanes(0)], at(dx=(1, 3, 2)[kind])
+        elif kind == 0:
             ref, device = wt.at[zof(i), y, half, lanes(0)], at(dy=1)
         elif kind == 1:
             ref, device = wt.at[zof(i), y, half, lanes(0)], at(dy=3)
@@ -205,7 +207,11 @@
         return remote(ref, ref, y_s.at[i, kind], y_r.at[i, kind], device)
 
     def x_move(i, kind):
-        if kind == 0:
+        if i == 7:
+            row = (y + (0, 0, 3, 1)[kind]) % 4
+            part = (pl.ds(0, HH), pl.ds(0, HH), pl.ds(0, HALF), pl.ds(HALF, HALF))[kind]
+            ref, device = wt.at[zof(i), row, half, part], at(dy=(1, 3, 1, 3)[kind])
+        elif kind == 0:
             ref, device = wt.at[zof(i), :, half, lanes(0)], at(dx=1)
         elif kind == 1:
             ref, device = wt.at[zof(i), :, half, lanes(0)], at(dx=3)
@@ -226,9 +232,12 @@
         return remote(ref, ref, f_s.at[r, kind], f_r.at[r, kind], device)
 
     def last_mirror(n):
-        rows = pl.ds(0, 2) if n == 3 else pl.ds(2, 2) if n == 4 else pl.ds(0, 4)
-        ref = wt.at[zof(7), rows, half, lanes((0, 3, 1, 2, 2)[n])]
-        return remote(ref, ref, m_s.at[7 + n], m_r.at[7 + n], partner)
+        if n < 5:
+            rows = pl.ds(0, 2) if n == 3 else pl.ds(2, 2) if n == 4 else pl.ds(0, 4)
+            ref = wt.at[zof(6), rows, half, lanes((0, 3, 1, 2, 2)[n])]
+        else:
+            ref = wt.at[zof(7), (y + (0, 3, 1, 2)[n - 5]) % 4, half]
+        return remote(ref, ref, m_s.at[6 + n], m_r.at[6 + n], partner)
 
     def mirror(i):
         ref = wt.at[zof(i), :, half]
@@ -313,18 +322,24 @@
             return
         x_move(i, 0).wait_recv()
         x_move(i, 2).start()
-        if i == 7:
-            last_mirror(1).start()
+        if i >= 6:
+            last_mirror(1 if i == 6 else 6).start()
         x_move(i, 1).wait_recv()
         x_move(i, 3).start()
-        if i == 7:
-            last_mirror(2).start()
+        if i >= 6:
+            last_mirror(2 if i == 6 else 7).start()
 
     def x_last(i):
         if i == 0:
             for r in range(4):
                 x_first(r, 2).wait_recv()
         elif i == 7:
+            last_mirror(5).start()
+            x_move(i, 2).wait_recv()
+            x_move(i, 3).wait_recv()
+            last_mirror(8).start()
+            return
+        elif i == 6:
             last_mirror(0).start()
             x_move(i, 2).wait_recv()
             last_mirror(3).start()
@@ -400,10 +415,10 @@
 
     def project(i, h):
         lane_half = pl.ds(h * HALF, HALF)
-        if h == 0 and i < 7:
+        if h == 0 and i < 6:
             mirror(i).wait_recv()
         elif h == 0:
-            for n in range(5):
+            for n in range(5) if i == 6 else range(5, 9):
                 last_mirror(n).wait_recv()
         block = wt[zof(i), :, :, lane_half].reshape(640, HALF)
         result = lax.dot_general(mixed[:, lane_half], block, NT, preferred_element_type=F32)
@@ -461,12 +476,12 @@
             y_move(i, kind).wait_send()
         for kind in range(4 if i else 0):
             x_move(i, kind).wait_send()
-        if i < 7:
+        if i < 6:
             mirror(i).wait_send()
     for r in range(4):
         for kind in range(3):
             x_first(r, kind).wait_send()
-    for n in range(5):
+    for n in range(9):
         last_mirror(n).wait_send()
 
 
@@ -514,8 +529,8 @@
             dma((8, 4)),
             dma((4, 3)),
             dma((4, 3)),
-            dma((12,)),
-            dma((12,)),
+            dma((15,)),
+            dma((15,)),
             dma((2,)),
         ],
         compiler_params=pltpu.CompilerParams(

time: 144 us -> 137 us (0.951)
  Pallas kernels: 140 us -> 132 us
    pallas_call x1, Pallas kernels: 140 us -> 132 us  [shards(): pl.pallas_call(kernel, out_shape=jax.ShapeDtypeStruct((256, D), BF16), in...]
where the time goes in v4:
time: 137 us; the launch traced here: 136 us
  Pallas kernels  132 us (96%)
  local copies, waits for them, and re-layouts  3.4 us (2%)
    pallas_call x1, Pallas kernels, shards(): pl.pallas_call(kernel, out_shape=jax.ShapeDtypeStruct((256, D), BF16), in...  132 us
    unnamed x1, local copies, waits for them, and re-layouts  3.4 us

profile of v4, /device:TPU:1, one launch (start us, length us, event | category | flops | bytes accessed | tf_op | source)
XLA Modules:
  0.0 135.5 jit_solution(17950688085084544851)
XLA Ops:
  0.0 132.1 %shard_map.91 = bf16[256,5120]{1,0:T(8,128)(2,1)} custom-call(bf16[256,2560]{1,0:T(8,128)(2,1)} %bitcast.11, bf16[256,2560]{1,0:T(8,128)(2,1)} %bitcast.12, bf16[256,2560]{1,0:T(8,128)(2,1)} %bitcast.13, s32[1,32]{1,0:T(1,128)} %bitcast.18, s32[9,32]{1,0:T(8,128)} %bitcast.17, s32[1,4]{1,0:T(1,128)} %bitcast.19, bf16[4,64,2560]{2,1,0:T(8,128)(2,1)} %bitcast.14, ...), custom_call_target="tpu_custom_call" | custom-call | flops 8999999488 | bytes 20000000 | tf_op jit(solution)/shard_map/pallas_call | solution.py:492
  132.1 3.4 %copy.11 = bf16[1,1,256,5120]{3,2,1,0:T(8,128)(2,1)} copy(bf16[1,1,256,5120]{3,2,1,0:T(8,128)(2,1)} %bitcast.10) | data formatting | bytes 5242880

commit v5 on v4

--- a/solution.py
+++ b/solution.py
@@ -14,8 +14,8 @@
 CACHE = 8
 HH = 2560
 HALF = 1280
-TEMPORAL_UNROLL = 5
-SCHEDULE = ('z1', 'z2', 'y0', 'b0', 'z3', 'z4', 'y1', 'k0', 'z5', 'z6', 'y2', 'z7', 'a0', 'x0', 'k1', 's0', 'y3', 's1', 'y7', 'y4', 's2', 'x1', 'y5', 's3', 'y6', 's4', 'x2', 'a1', 't0', 'x3', 'x4', 'x5', 'x7', 'x6', 'l0', 'l1', 'l2', 'l3', 'l7', 'l4', 'l5', 't1', 'l6', 'c0', 'p0', 'p1', 'p2', 'p3', 'p4', 'p5', 'p7', 'p6', 'c1', 'p10', 'p11', 'p12', 'p13', 'p14', 'p15', 'p17', 'p16')
+TEMPORAL_UNROLL = 10
+SCHEDULE = ('z1', 'z2', 'y0', 'z3', 'z4', 'b0', 'y1', 'z5', 'z6', 'k0', 'y2', 'z7', 'a0', 'x0', 'k1', 's0', 'y3', 's1', 'y7', 'y4', 's2', 'x1', 'y5', 's3', 'y6', 's4', 'x2', 'a1', 't0', 'x3', 'x4', 'x5', 'x7', 'x6', 'l0', 'l1', 'l2', 'l3', 'l7', 'l4', 'l5', 't1', 'l6', 'c0', 'p0', 'p1', 'p2', 'p3', 'p4', 'p5', 'p7', 'p6', 'c1', 'p10', 'p11', 'p12', 'p13', 'p14', 'p15', 'p17', 'p16')
 D = 5120
 BF16 = jnp.bfloat16
 F32 = jnp.float32

time: 137 us -> 137 us (level)
  no operation moved by 1% of the time
where the time goes in v5:
time: 137 us; the launch traced here: 136 us
  Pallas kernels  132 us (96%)
  local copies, waits for them, and re-layouts  3.4 us (2%)
    pallas_call x1, Pallas kernels, shards(): pl.pallas_call(kernel, out_shape=jax.ShapeDtypeStruct((256, D), BF16), in...  132 us
    unnamed x1, local copies, waits for them, and re-layouts  3.4 us

profile of v5, /device:TPU:1, one launch (start us, length us, event | category | flops | bytes accessed | tf_op | source)
XLA Modules:
  0.0 135.6 jit_solution(7959009780629419369)
XLA Ops:
  0.0 132.1 %shard_map.91 = bf16[256,5120]{1,0:T(8,128)(2,1)} custom-call(bf16[256,2560]{1,0:T(8,128)(2,1)} %bitcast.11, bf16[256,2560]{1,0:T(8,128)(2,1)} %bitcast.12, bf16[256,2560]{1,0:T(8,128)(2,1)} %bitcast.13, s32[1,32]{1,0:T(1,128)} %bitcast.18, s32[9,32]{1,0:T(8,128)} %bitcast.17, s32[1,4]{1,0:T(1,128)} %bitcast.19, bf16[4,64,2560]{2,1,0:T(8,128)(2,1)} %bitcast.14, ...), custom_call_target="tpu_custom_call" | custom-call | flops 8999999488 | bytes 20000000 | tf_op jit(solution)/shard_map/pallas_call | solution.py:492
  132.2 3.4 %copy.11 = bf16[1,1,256,5120]{3,2,1,0:T(8,128)(2,1)} copy(bf16[1,1,256,5120]{3,2,1,0:T(8,128)(2,1)} %bitcast.10) | data formatting | bytes 5242880
